TPU v7x, 256 devices: a whole 4x4x8 slice. The times are simulated.
256 devices in a mesh: sp: 64 (over z, x, core), batch: 4 (over y).
Axes of the slice: x: 4, y: 4, z: 8, core: 2. Of those that a mesh axis runs over, the one named last changes fastest.
Arguments:
- lifted_field: float32 [128, 128, 8192], P('batch', 'sp'), parts along dimension 0, may hold values from -6 to 6
- target_field: float32 [128, 32768], P('sp', 'batch'), parts along dimension 1, may hold values from -6 to 6
- spectral_one: float32 [2, 32, 512, 1024], P(None, None, 'sp'), may hold values from -5 to 5
- spectral_two: float32 [2, 32, 512, 1024], P(None, None, 'sp'), may hold values from -5 to 5
- pointwise_one: float32 [32, 32], replicated, may hold values from -1 to 1
- layer_bias_one: float32 [32], replicated, may hold values from -3 to 3
- pointwise_two: float32 [32, 32], replicated, may hold values from -1 to 1
- layer_bias_two: float32 [32], replicated, may hold values from -3 to 3
- hidden_weight: float32 [128, 32], replicated, may hold values from -1 to 1
- hidden_bias: float32 [128], replicated, may hold values from -3 to 3
- output_weight: float32 [128], replicated, may hold values from -4 to 4
Outputs:
- gradient_one: float32 [8, 32, 512, 1024], P('batch', None, 'sp'), parts along dimension 0
- gradient_two: float32 [8, 32, 512, 1024], P('batch', None, 'sp'), parts along dimension 0
There are 4 independent parts, one for each index of `batch`. A program takes and returns all parts, laid end to end along the dimension named above; an argument that names none is the same for every part. Nothing has to cross between parts.
All inputs are finite; a program needn't handle non-finite values.
Results may differ from a plain program's by a relative error of at most 0.00018.
Values sent between devices are 32-bit elements; how exact they have to be, the bound alone decides.
No kernel may reach another device: no remote copies, remote signals or barrier semaphores. Data moves between devices by JAX's collectives and lax.ppermute only.
A program may use at most 128 MiB of HBM per device.

v0:
```python
import math

import jax
import jax.numpy as jnp
from jax import lax
from jax.sharding import PartitionSpec as P

NX = 128
NY = 128
NZ = 64
KX = 32
KY = 32
KZ = 16


precise = lax.Precision.HIGHEST


def product(form, left_operand, right_operand):
    return jnp.einsum(
        form, left_operand, right_operand, precision=precise, preferred_element_type=jnp.float32
    )


def centred(number, length):
    indices = jnp.arange(number, dtype=jnp.int32)
    return jnp.where(indices < number // 2, indices, length - number + indices)


def phases(length, places, frequency):
    cycles = places[:, None] * frequency[None, :] % length
    angles = cycles.astype(jnp.float32) * (2.0 * math.pi / length)
    return (jnp.cos(angles), jnp.sin(angles))


def forward_mixer(length, places, number):
    cosine_part, sine_part = phases(length, places, centred(number, length))
    return jnp.stack(
        [jnp.stack([cosine_part, -sine_part], 1), jnp.stack([sine_part, cosine_part], 1)], 1
    )


def inverse_mixer(length, places, number):
    cosine_part, sine_part = phases(length, places, centred(number, length))
    cosine_turned = cosine_part.T
    sine_turned = sine_part.T
    return jnp.stack(
        [jnp.stack([cosine_turned, sine_turned], 0), jnp.stack([-sine_turned, cosine_turned], 0)], 0
    )


def depth_table(doubled):
    frequency = jnp.arange(KZ, dtype=jnp.int32)
    cosine_part, sine_part = phases(NZ, jnp.arange(NZ, dtype=jnp.int32), frequency)
    if doubled:
        factor = jnp.where(frequency > 0, 2.0, 1.0)
    else:
        factor = jnp.ones((KZ,), jnp.float32)
    factor = factor / math.sqrt(NX * NY * NZ)
    return jnp.stack([cosine_part * factor, -sine_part * factor], 1)


def to_modes(field_slab, doubled):
    channels, rows_here = (field_slab.shape[0], field_slab.shape[1])
    depth_spectra = product(
        "cryz,zpk->crypk", field_slab.reshape(channels, rows_here, NY, NZ), depth_table(doubled)
    )
    across_mixer = forward_mixer(NY, jnp.arange(NY, dtype=jnp.int32), KY)
    across_spectra = product("crypk,ypsq->rsqkc", depth_spectra, across_mixer)
    slab_data = across_spectra.reshape(rows_here, 2, KY * KZ * channels)
    pencil = lax.all_to_all(slab_data, "sp", split_axis=2, concat_axis=0, tiled=True)
    first_mixer = forward_mixer(NX, jnp.arange(NX, dtype=jnp.int32), KX)
    modes_here = pencil.shape[2] // channels
    spectrum = product("npj,npsx->sxj", pencil, first_mixer)
    return spectrum.reshape(2, KX, modes_here, channels)


def to_cells(spectrum, doubled):
    modes_here, channels = (spectrum.shape[2], spectrum.shape[3])
    first_mixer = inverse_mixer(NX, jnp.arange(NX, dtype=jnp.int32), KX)
    flat_spectrum = spectrum.reshape(2, KX, modes_here * channels)
    pencil = product("pxj,psxn->nsj", flat_spectrum, first_mixer)
    slab_data = lax.all_to_all(pencil, "sp", split_axis=0, concat_axis=2, tiled=True)
    rows_here = slab_data.shape[0]
    blocks = slab_data.reshape(rows_here, 2, KY, KZ, channels)
    across_mixer = inverse_mixer(NY, jnp.arange(NY, dtype=jnp.int32), KY)
    across_cells = product("rpqkc,psqy->crysk", blocks, jnp.transpose(across_mixer, (0, 1, 2, 3)))
    rebuilt = product("crysk,zsk->cryz", across_cells, depth_table(doubled))
    return rebuilt.reshape(channels, rows_here, NY * NZ)


def weights_grid(spectral, channels):
    return spectral.reshape(spectral.shape[:3] + (channels, channels))


def apply_modes(spectrum, spectral):
    channels = spectrum.shape[3]
    weights = weights_grid(spectral, channels)
    real_out = product("xmi,xmio->xmo", spectrum[0], weights[0]) - product(
        "xmi,xmio->xmo", spectrum[1], weights[1]
    )
    imag_out = product("xmi,xmio->xmo", spectrum[0], weights[1]) + product(
        "xmi,xmio->xmo", spectrum[1], weights[0]
    )
    return jnp.stack([real_out, imag_out], 0)


def adjoint_modes(spectrum, spectral):
    channels = spectrum.shape[3]
    weights = weights_grid(spectral, channels)
    real_out = product("xmo,xmio->xmi", spectrum[0], weights[0]) + product(
        "xmo,xmio->xmi", spectrum[1], weights[1]
    )
    imag_out = product("xmo,xmio->xmi", spectrum[1], weights[0]) - product(
        "xmo,xmio->xmi", spectrum[0], weights[1]
    )
    return jnp.stack([real_out, imag_out], 0)


def weight_gradient(forward_spectrum, back_spectrum):
    channels = forward_spectrum.shape[3]
    real_grad = product("xmi,xmo->xmio", forward_spectrum[0], back_spectrum[0]) + product(
        "xmi,xmo->xmio", forward_spectrum[1], back_spectrum[1]
    )
    imag_grad = product("xmi,xmo->xmio", forward_spectrum[0], back_spectrum[1]) - product(
        "xmi,xmo->xmio", forward_spectrum[1], back_spectrum[0]
    )
    stacked = jnp.stack([real_grad, imag_grad], 0)
    return stacked.reshape(stacked.shape[:3] + (channels * channels,))


def gelu_back(pre_gelu, cotangent):
    _, pullback = jax.vjp(jax.nn.gelu, pre_gelu)
    return pullback(cotangent)[0]


def shards(
    lifted_field,
    target_field,
    spectral_one,
    spectral_two,
    pointwise_one,
    layer_bias_one,
    pointwise_two,
    layer_bias_two,
    hidden_weight,
    hidden_bias,
    output_weight,
):

    def apply_layer(layer_input, spectral, pointwise, layer_bias):
        spectrum_in = to_modes(layer_input, False)
        spectrum_out = apply_modes(spectrum_in, spectral)
        local_term = product("oi,icn->ocn", pointwise, layer_input) + layer_bias[:, None, None]
        pre_gelu = to_cells(spectrum_out, True) + local_term
        return (pre_gelu, spectrum_in)

    pre_one, spectrum_one = apply_layer(lifted_field, spectral_one, pointwise_one, layer_bias_one)
    state_one = jax.nn.gelu(pre_one)
    pre_two, spectrum_two = apply_layer(state_one, spectral_two, pointwise_two, layer_bias_two)
    state_two = jax.nn.gelu(pre_two)
    hidden_pre = product("hi,icn->hcn", hidden_weight, state_two) + hidden_bias[:, None, None]
    predicted = product("h,hcn->cn", output_weight, jax.nn.gelu(hidden_pre))
    misfit = predicted - target_field
    back_hidden = gelu_back(hidden_pre, output_weight[:, None, None] * misfit[None])
    back_two = gelu_back(pre_two, product("hi,hcn->icn", hidden_weight, back_hidden))
    back_spectrum = to_modes(back_two, True)
    gradient_two = weight_gradient(spectrum_two, back_spectrum)
    adjoint_spectrum = adjoint_modes(back_spectrum, spectral_two)
    local_back = product("oi,ocn->icn", pointwise_two, back_two)
    back_state = local_back + to_cells(adjoint_spectrum, False)
    back_one = gelu_back(pre_one, back_state)
    first_spectrum = to_modes(back_one, True)
    gradient_one = weight_gradient(spectrum_one, first_spectrum)
    return (gradient_one, gradient_two)


def solution(mesh):
    in_specs = (
        P("batch", "sp", None),
        P("sp", "batch"),
        P(None, None, "sp", None),
        P(None, None, "sp", None),
        P(),
        P(),
        P(),
        P(),
        P(),
        P(),
        P(),
    )
    out_specs = (P("batch", None, "sp", None), P("batch", None, "sp", None))
    return jax.shard_map(shards, mesh=mesh, in_specs=in_specs, out_specs=out_specs, check_vma=False)
```

profile of v0, /device:TPU:1, one launch (start us, length us, event | category | flops | bytes accessed | tf_op | source)
XLA Modules:
  0.0 715.7 jit_solution(1208495478245337952)
XLA Ops:
  15.2 17.6 %copy.137 = f32[2,2,32,16,32]{1,0,4,3,2:T(2,128)} copy(f32[2,2,32,16,32]{4,2,3,0,1:T(8,128)S(1)} %convolution_bitcast_fusion.11) | data formatting | bytes 524288 | tf_op jit(solution)/shard_map/reshape | solution.py:70
  32.8 25.8 %reshape.578 = f32[64,1,1024]{2,1,0:T(1,128)} reshape(f32[16384,2,2]{2,1,0:T(2,128)} %bitcast.342) | data formatting | bytes 524288
  58.6 13.6 %all-to-all-start = ((f32[64,1,1024]{2,1,0:T(1,128)}), f32[64,1,1024]{2,1,0:T(1,128)S(1)}, u32[]{:S(2)}, u32[]{:S(2)}) async-start(f32[64,1,1024]{2,1,0:T(1,128)} %reshape.578), calls=%async_computation | async-start | bytes 524288 | tf_op jit(solution)/shard_map/all_to_all | solution.py:71
  87.0 27.0 %reshape.579 = f32[16384,2,2]{2,1,0:T(2,128)} reshape(f32[64,1024]{1,0:T(8,128)S(1)} %reduce) | data formatting | bytes 524288
  114.1 13.4 %copy.138 = f32[2,2,64,256]{3,2,1,0:T(8,128)S(1)} copy(f32[2,2,64,256]{1,0,3,2:T(2,128)} %bitcast.343) | data formatting | bytes 524288 | tf_op jit(solution)/shard_map/all_to_all | solution.py:71
  150.6 13.2 %all-to-all-done.1 = f32[128,2,256]{2,1,0:T(2,128)S(1)} async-done(((f32[128,2,256]{2,1,0:T(2,128)}), f32[128,2,256]{2,1,0:T(2,128)S(1)}, u32[]{:S(2)}, u32[]{:S(2)}) %all-to-all-start.1) | async-done | bytes 262176 | tf_op jit(solution)/shard_map/all_to_all | solution.py:83
  200.4 17.6 %copy.144 = f32[2,2,32,16,32]{1,0,4,3,2:T(2,128)} copy(f32[2,2,32,16,32]{4,2,3,0,1:T(8,128)S(1)} %convolution_bitcast_fusion.9) | data formatting | bytes 524288 | tf_op jit(solution)/shard_map/reshape | solution.py:70
  218.1 25.8 %reshape.580 = f32[64,1,1024]{2,1,0:T(1,128)} reshape(f32[16384,2,2]{2,1,0:T(2,128)} %bitcast.344) | data formatting | bytes 524288
  263.1 27.0 %reshape.581 = f32[16384,2,2]{2,1,0:T(2,128)} reshape(f32[64,1024]{1,0:T(8,128)S(1)} %reduce.1) | data formatting | bytes 524288
  290.1 13.4 %copy.145 = f32[2,2,64,256]{3,2,1,0:T(8,128)S(1)} copy(f32[2,2,64,256]{1,0,3,2:T(2,128)} %bitcast.345) | data formatting | bytes 524288 | tf_op jit(solution)/shard_map/all_to_all | solution.py:71
  321.1 17.7 %all_to_all.117 = f32[128,2,256]{2,1,0:T(2,128)S(1)} all-to-all(f32[128,2,256]{2,1,0:T(2,128)S(1)} %copy.60), channel_id=1, replica_groups=mesh['sp'=64,'batch'=4] {'sp'}, dimensions={0} | all-to-all | bytes 524288 | tf_op jit(solution)/shard_map/all_to_all | solution.py:83
  357.4 13.4 %fusion = f32[128,2,8192]{0,2,1:T(8,128)S(1)} fusion(f32[128]{0:T(128)S(1)} %copy-done.15, f32[32,2,8192]{2,0,1:T(8,128)S(1)} %fusion.3, f32[128,32]{0,1:T(8,128)S(1)} %copy-done), kind=kOutput, calls=%fused_computation.5 | convolution fusion | flops 811597824 | bytes 10502656 | tf_op jit(solution)/shard_map/hi,icn->hcn/dot_general | solution.py:20
  370.9 9.8 %fusion.21 = f32[1,2,8192]{2,0,1:T(1,128)S(1)} fusion(f32[128,2,8192]{0,2,1:T(8,128)S(1)} %fusion, f32[128]{0:T(128)S(1)} %copy-done.17), kind=kOutput, calls=%fused_computation.27 | convolution fusion | flops 41943040 | bytes 8454656 | tf_op jit(solution)/shard_map/h,hcn->cn/dot_general | solution.py:20
  380.8 14.1 %fusion.60 = f32[32,2,8192]{2,0,1:T(8,128)S(1)} fusion(f32[32,2,8192]{2,0,1:T(8,128)S(1)} %fusion.3, f32[128,2,8192]{0,2,1:T(8,128)S(1)} %fusion, f32[2,8192]{1,0:T(2,128)S(1)} %bitcast_subtract_fusion, f32[128]{0:T(128)S(1)} %copy-done.17, f32[128,32]{0,1:T(8,128)S(1)} %copy-done), kind=kOutput, calls=%fused_computation.75 | convolution fusion | flops 857210880 | bytes 12665344 | tf_op jit(solution)/shard_map/hi,hcn->icn/dot_general | solution.py:20
  407.2 17.6 %copy.152 = f32[2,2,32,16,32]{1,0,4,3,2:T(2,128)} copy(f32[2,2,32,16,32]{4,2,3,0,1:T(8,128)S(1)} %convolution_bitcast_fusion.7) | data formatting | bytes 524288 | tf_op jit(solution)/shard_map/reshape | solution.py:70
  424.8 25.2 %reshape.582 = f32[64,1,1024]{2,1,0:T(1,128)S(1)} reshape(f32[16384,2,2]{2,1,0:T(2,128)} %bitcast.346) | data formatting | bytes 524288
  450.0 17.9 %all_to_all.118 = f32[64,1,1024]{2,1,0:T(1,128)S(1)} all-to-all(f32[64,1,1024]{2,1,0:T(1,128)S(1)} %reshape.582), channel_id=1, replica_groups=mesh['sp'=64,'batch'=4] {'sp'}, dimensions={0} | all-to-all | bytes 524288 | tf_op jit(solution)/shard_map/all_to_all | solution.py:71
  469.1 27.0 %reshape.583 = f32[16384,2,2]{2,1,0:T(2,128)} reshape(f32[64,1024]{1,0:T(8,128)S(1)} %reduce.2) | data formatting | bytes 524288
  496.2 13.4 %copy.153 = f32[2,2,64,256]{3,2,1,0:T(8,128)S(1)} copy(f32[2,2,64,256]{1,0,3,2:T(2,128)} %bitcast.347) | data formatting | bytes 524288 | tf_op jit(solution)/shard_map/all_to_all | solution.py:71
  548.3 12.5 %all-to-all-done.5 = f32[128,2,256]{2,1,0:T(2,128)S(1)} async-done(((f32[128,2,256]{2,1,0:T(2,128)}), f32[128,2,256]{2,1,0:T(2,128)S(1)}, u32[]{:S(2)}, u32[]{:S(2)}) %all-to-all-start.5) | async-done | bytes 262176 | tf_op jit(solution)/shard_map/all_to_all | solution.py:83
  597.0 17.6 %copy.159 = f32[2,2,32,16,32]{1,0,4,3,2:T(2,128)} copy(f32[2,2,32,16,32]{4,2,3,0,1:T(8,128)S(1)} %convolution_bitcast_fusion.5) | data formatting | bytes 524288 | tf_op jit(solution)/shard_map/reshape | solution.py:70
  614.6 25.8 %reshape.584 = f32[64,1,1024]{2,1,0:T(1,128)} reshape(f32[16384,2,2]{2,1,0:T(2,128)} %bitcast.348) | data formatting | bytes 524288
  660.4 27.0 %reshape.585 = f32[16384,2,2]{2,1,0:T(2,128)} reshape(f32[64,1024]{1,0:T(8,128)S(1)} %reduce.3) | data formatting | bytes 524288
  687.4 13.4 %copy.160 = f32[2,2,64,256]{3,2,1,0:T(8,128)S(1)} copy(f32[2,2,64,256]{1,0,3,2:T(2,128)} %bitcast.349) | data formatting | bytes 524288 | tf_op jit(solution)/shard_map/all_to_all | solution.py:71
  (164 shorter events, 266.7 us)
Async XLA Ops:
  0.6 356.8 %copy-start = (f32[128,32]{0,1:T(8,128)S(1)}, f32[128,32]{0,1:T(8,128)}, u32[]{:S(2)}) copy-start(f32[128,32]{0,1:T(8,128)} %param.19) | copy-start | bytes 49156
  58.6 26.7 %all-to-all-start = ((f32[64,1,1024]{2,1,0:T(1,128)}), f32[64,1,1024]{2,1,0:T(1,128)S(1)}, u32[]{:S(2)}, u32[]{:S(2)}) async-start(f32[64,1,1024]{2,1,0:T(1,128)} %reshape.578), calls=%async_computation | async-start | bytes 524288 | tf_op jit(solution)/shard_map/all_to_all | solution.py:71
  128.3 5.5 copy-start.7
  133.9 6.9 copy-start.6
  145.8 18.0 %all-to-all-start.1 = ((f32[128,2,256]{2,1,0:T(2,128)}), f32[128,2,256]{2,1,0:T(2,128)S(1)}, u32[]{:S(2)}, u32[]{:S(2)}) async-start(f32[128,2,256]{2,1,0:T(2,128)} %copy.49), calls=%async_computation.1 | async-start | bytes 524288 | tf_op jit(solution)/shard_map/all_to_all | solution.py:83
  174.3 4.9 copy-start.8
  174.3 4.9 copy-start.12
  174.3 4.9 copy-start.16
  243.9 17.9 %all-to-all-start.2 = ((f32[64,1,1024]{2,1,0:T(1,128)}), f32[64,1,1024]{2,1,0:T(1,128)S(1)}, u32[]{:S(2)}, u32[]{:S(2)}) async-start(f32[64,1,1024]{2,1,0:T(1,128)} %reshape.580), calls=%async_computation.2 | async-start | bytes 524288 | tf_op jit(solution)/shard_map/all_to_all | solution.py:71
  304.4 5.5 copy-start.4
  309.9 6.9 copy-start.2
  349.4 3.7 copy-start.13
  349.4 3.7 copy-start.14
  353.1 4.3 copy-start.15
  357.4 13.4 %copy-start.17 = (f32[128]{0:T(128)S(1)}, f32[128]{0:T(128)}, u32[]{:S(2)}) copy-start(f32[128]{0:T(128)} %param.21) | copy-start | bytes 1540
  370.9 9.8 %copy-start.11 = (f32[2,8192]{1,0:T(2,128)S(1)}, f32[2,8192]{1,0:T(2,128)}, u32[]{:S(2)}) copy-start(f32[2,8192]{1,0:T(2,128)} %param.12) | copy-start | bytes 196612
  394.9 3.0 copy-start.10
  510.3 8.5 %copy-start.5 = (f32[32,8,32,32]{3,2,1,0:T(8,128)S(1)}, f32[32,8,32,32]{3,2,1,0:T(8,128)}, u32[]{:S(2)}) copy-start(f32[32,8,32,32]{3,2,1,0:T(8,128)} %squeeze.31) | copy-start | bytes 3145732
  525.6 9.0 %copy-start.3 = (f32[32,8,32,32]{3,2,1,0:T(8,128)S(1)}, f32[32,8,32,32]{3,2,1,0:T(8,128)}, u32[]{:S(2)}) copy-start(f32[32,8,32,32]{3,2,1,0:T(8,128)} %squeeze.29) | copy-start | bytes 3145732
  542.7 18.0 %all-to-all-start.5 = ((f32[128,2,256]{2,1,0:T(2,128)}), f32[128,2,256]{2,1,0:T(2,128)S(1)}, u32[]{:S(2)}, u32[]{:S(2)}) async-start(f32[128,2,256]{2,1,0:T(2,128)} %copy.72), calls=%async_computation.5 | async-start | bytes 524288 | tf_op jit(solution)/shard_map/all_to_all | solution.py:83
  571.3 4.9 copy-start.9
  640.4 18.7 %all-to-all-start.6 = ((f32[64,1,1024]{2,1,0:T(1,128)}), f32[64,1,1024]{2,1,0:T(1,128)S(1)}, u32[]{:S(2)}, u32[]{:S(2)}) async-start(f32[64,1,1024]{2,1,0:T(1,128)} %reshape.584), calls=%async_computation.6 | async-start | bytes 524288 | tf_op jit(solution)/shard_map/all_to_all | solution.py:71
  710.0 5.2 copy-start.1
where the time goes:
time: 724 us; the launch traced here: 716 us
  local copies, waits for them, and re-layouts  405 us (56%)
  matrix products  185 us (26%)
  waiting for transfers between devices  37.3 us (5%)
  blocking collectives  35.5 us (5%)
  starting transfers between devices  33.2 us (5%)
  other arithmetic  17.8 us (2%)
    unnamed x44, local copies, waits for them, and re-layouts  211 us
    dot_general x39, matrix products, product(): jnp.einsum(form, left_operand, right_operand, precision=precise, preferre...  185 us
    reshape x4, local copies, waits for them, and re-layouts, to_modes(): slab_data = across_spectra.reshape(rows_here, 2, KY * KZ * channels)  70.4 us
    all_to_all x13, local copies, waits for them, and re-layouts, to_modes(): lax.all_to_all(slab_data, 'sp', split_axis=2, concat_axis=0, tiled=True)  55.7 us
    all_to_all x2, waiting for transfers between devices, to_cells(): lax.all_to_all(pencil, 'sp', split_axis=0, concat_axis=2, tiled=True)  25.6 us
    all_to_all x3, starting transfers between devices, to_modes(): lax.all_to_all(slab_data, 'sp', split_axis=2, concat_axis=0, tiled=True)  23.4 us
    all_to_all x1, blocking collectives, to_modes(): lax.all_to_all(slab_data, 'sp', split_axis=2, concat_axis=0, tiled=True)  17.9 us
    all_to_all x1, blocking collectives, to_cells(): lax.all_to_all(pencil, 'sp', split_axis=0, concat_axis=2, tiled=True)  17.7 us
  transfers between devices with their start and end apart: 5, of which 4 were waited for; matrix products, arithmetic and copies ran while one was open for 4% of the time, Pallas kernels for 0%

commit v1 on v0

v1 whole, which is shorter than its diff:
```python
import jax
import jax.numpy as jnp
import ml_dtypes
import numpy as np
from jax import lax
from jax.experimental import pallas as pl
from jax.experimental.pallas import tpu as pltpu
from jax.sharding import PartitionSpec as P

W = 32
H = 128
NX = 128
NY = 128
NZ = 64
KX = 32
KY = 32
KZ = 16

f32 = jnp.float32
bf16 = jnp.bfloat16
ROOT = 0.7978845608028654
CUBE = 0.044715 * ROOT


def centred(number, length):
    indices = np.arange(number)
    return np.where(indices < number // 2, indices, length - number + indices)


def two_parts(table):
    high = table.astype(ml_dtypes.bfloat16)
    low = (table - high.astype(np.float64)).astype(ml_dtypes.bfloat16)
    return high, low


def across_table():
    y = 2 * np.arange(64)[None, :] + np.arange(2)[:, None]
    angle = 2 * np.pi * (centred(KY, NY)[:, None, None] * y[None] % NY) / NY
    waves = np.stack([np.cos(angle), -np.sin(angle)])
    return np.einsum("skab,rt->srkabt", waves, np.eye(2)).reshape(128, 256)


def rotation(angle):
    cosine, sine = np.cos(angle), np.sin(angle)
    return np.stack([np.stack([cosine, -sine]), np.stack([sine, cosine])])


def depth_table(channel_major):
    angle = 2 * np.pi * (np.arange(NZ)[:, None] * np.arange(KZ)[None] % NZ) / NZ
    form = "zk,cd->czkd" if channel_major else "zk,cd->zckd"
    return [np.einsum(form, wave(angle), np.eye(16)).reshape(1024, 256) for wave in (np.cos, np.sin)]


def first_table():
    places = 2 * np.arange(64)[:, None] + np.arange(2)[None]
    angle = 2 * np.pi * (centred(KX, NX)[:, None, None] * places[None] % NX) / NX
    table = np.einsum("stkdr,gh->gtkdrsh", rotation(angle), np.eye(2))
    return table.reshape(128, 512) / 1024.0


def selectors():
    eye16, eye32 = np.eye(16), np.eye(32)
    lanes = np.zeros((128, 32))
    lanes[:32] = eye32
    spread = np.einsum("li,o->lio", lanes, np.ones(32)).reshape(128, 1024)
    tile = np.einsum("lo,i->lio", lanes, np.ones(4)).reshape(128, 128)
    halves = eye32.reshape(32, 2, 16)
    gather = np.einsum("i,ogc,k->iogkc", np.ones(4), halves, np.ones(8)).reshape(128, 256)
    gather_rows = np.einsum("igc,o,k->iogkc", halves, np.ones(32), np.ones(8)).reshape(1024, 256)
    return [part.astype(ml_dtypes.bfloat16) for part in (spread, tile, gather, gather_rows)]


def head_selectors():
    one = ml_dtypes.bfloat16
    channels = np.einsum("z,igc->gzci", np.ones(8), np.eye(32).reshape(32, 2, 16)).reshape(256, 32)
    hidden = np.einsum("hbu,z->hbzu", np.eye(128).reshape(128, 8, 16), np.ones(8)).reshape(128, 1024)
    ones = np.einsum("zy,uc->zuyc", np.eye(8), np.ones((16, 16))).reshape(128, 128)
    cells = np.einsum("ab,zy,c->bzayc", np.eye(2), np.eye(64), np.ones(16)).reshape(128, 2048)
    return channels.astype(one), hidden.astype(one), ones.astype(one), cells.astype(one)


def turn_table():
    return np.einsum("zy,cd->czyd", np.eye(64), np.eye(16)).reshape(1024, 1024).astype(ml_dtypes.bfloat16)


def split(values):
    high = values.astype(bf16)
    return high, (values - high.astype(f32)).astype(bf16)


def dot(left, right):
    return lax.dot_general(left, right, (((1,), (0,)), ((), ())), preferred_element_type=f32)


def dot_t(left, right):
    return lax.dot_general(left, right, (((1,), (1,)), ((), ())), preferred_element_type=f32)


def dot3(left, right, product=dot):
    return product(left[0], right[0]) + (product(left[1], right[0]) + product(left[0], right[1]))


def run(body, name, flops, near, far, outs, scratch):
    leaving = [k for k, out in enumerate(outs) if out[2] == "far"]

    def kernel(*refs):
        refs = list(refs)
        take = lambda count: [refs.pop(0) for _ in range(count)]
        near_refs, far_refs, out_refs = take(len(near)), take(len(far)), take(len(outs))
        copied, filled = take(len(far)), take(len(leaving))
        scratch_refs = take(len(scratch))
        arrived, left = refs
        copies = [pltpu.make_async_copy(a, b, arrived.at[k]) for k, (a, b) in enumerate(zip(far_refs, copied))]
        for copy in copies:
            copy.start()
        waited, started = set(), []

        def fetch(k):
            if k not in waited:
                copies[k].wait()
                waited.add(k)
            return copied[k]

        def put(k):
            index = leaving.index(k)
            copy = pltpu.make_async_copy(filled[index], out_refs[k], left.at[index])
            copy.start()
            started.append(copy)

        shown = [filled[leaving.index(k)] if k in leaving else out for k, out in enumerate(out_refs)]
        body(near_refs, fetch, shown, put, scratch_refs)
        for k in range(len(far)):
            fetch(k)
        for copy in started:
            copy.wait()

    far = [pltpu.with_memory_space_constraint(o, pltpu.HBM) for o in far]
    vmem, hbm = pl.BlockSpec(memory_space=pltpu.VMEM), pl.BlockSpec(memory_space=pltpu.HBM)
    moved = sum(o.size * o.dtype.itemsize for o in (*near, *far))
    return pl.pallas_call(
        kernel,
        in_specs=[vmem] * len(near) + [hbm] * len(far),
        out_specs=[hbm if out[2] == "far" else vmem for out in outs],
        out_shape=[pltpu.HBM(out[0], out[1]) if out[2] == "far" else jax.ShapeDtypeStruct(out[0], out[1]) for out in outs],
        scratch_shapes=[pltpu.VMEM(o.shape, o.dtype) for o in far]
        + [pltpu.VMEM(outs[k][0], outs[k][1]) for k in leaving]
        + scratch
        + [pltpu.SemaphoreType.DMA((max(1, len(far)),)), pltpu.SemaphoreType.DMA((max(1, len(leaving)),))],
        name=name,
        cost_estimate=pl.CostEstimate(flops=flops, bytes_accessed=int(moved), transcendentals=0),
        compiler_params=pltpu.CompilerParams(vmem_limit_bytes=48 * 1024 * 1024),
    )(*near, *far)


def spectra_of(turned, depth):
    rows = [turned[s * 64 : s * 64 + 64, g * 1024 : g * 1024 + 1024] for s in range(2) for g in range(2)]
    left = split(jnp.concatenate(rows, 0))
    even = dot3(left, (depth[0][...], depth[1][...]))
    odd = dot3(left, (depth[2][...], depth[3][...]))
    return even[:128] + odd[128:], even[128:] - odd[:128]


def place_modes(spectra, send_ref):
    for p in range(2):
        for g in range(2):
            for r in range(2):
                for kzh in range(2):
                    row = g * 64 + r * 32
                    send_ref[pl.ds(kzh * 8 + r * 4 + p * 2 + g, 32, stride=16), :] = spectra[p][
                        row : row + 32, kzh * 128 : kzh * 128 + 128
                    ]


def send_modes(parts, across, depth, send_ref):
    turned = dot3((across[0][...], across[1][...]), parts)
    place_modes(spectra_of(turned, depth), send_ref)


def taken_rows(recv_ref):
    rows = []
    for p in range(2):
        for g in range(2):
            for r in range(2):
                pieces = [recv_ref[pl.ds(kzh * 8 + r * 4 + p * 2 + g, 32, stride=16), :] for kzh in range(2)]
                rows.append(jnp.concatenate(pieces, 1))
    return split(jnp.concatenate(rows, 0))


def cells_from(recv_ref, back, depth):
    left = taken_rows(recv_ref)
    depth = [depth(k) for k in range(4)]
    even = dot3(left, (depth[0][...], depth[1][...]), dot_t)
    odd = dot3(left, (depth[2][...], depth[3][...]), dot_t)
    real, imag = even[:128] - odd[128:], odd[:128] + even[128:]
    rows = [jnp.concatenate([part[:64], part[64:]], 1) for part in (real, imag)]
    back = [back(k) for k in range(2)]
    return dot3((back[0][...], back[1][...]), split(jnp.concatenate(rows, 0)))


def plain_rows(field_ref, g):
    low_rows, high_rows = [], []
    lane = lax.broadcasted_iota(jnp.int32, (128, 128), 1) < 64
    for pair in range(8):
        first = field_ref[g * 16 + 2 * pair]
        second = field_ref[g * 16 + 2 * pair + 1]
        low_rows.append(jnp.where(lane, first, pltpu.roll(second, 64, 1)))
        high_rows.append(jnp.where(lane, pltpu.roll(first, 64, 1), second))
    return jnp.concatenate([jnp.concatenate(low_rows, 1), jnp.concatenate(high_rows, 1)], 0)


def lift_body(near, fetch, outs, put, scratch):
    field_ref = fetch(0)
    parts = [split(plain_rows(field_ref, g)) for g in range(2)]
    parts = tuple(jnp.concatenate([parts[0][k], parts[1][k]], 1) for k in range(2))
    turned = dot3((fetch(1)[...], fetch(2)[...]), parts)
    place_modes(spectra_of(turned, [fetch(k) for k in range(3, 7)]), outs[0])


def point_chunks(parts_at, mix, bias, out_ref):
    for q in range(8):
        mixed = dot3(parts_at(q), mix) + bias
        out_ref[:, q * 128 : q * 128 + 128] = mixed[:, :128]
        out_ref[:, 1024 + q * 128 : 1152 + q * 128] = mixed[:, 128:]


def both(value, q):
    return jnp.concatenate([value[:, q * 128 : q * 128 + 128], value[:, 1024 + q * 128 : 1152 + q * 128]], 1)


def lift_point_body(near, fetch, outs, put, scratch):
    turned = []
    for g in range(2):
        high, low = split(plain_rows(fetch(0), g))
        turned.append((dot(high, fetch(1)[...]).astype(bf16), dot(low, fetch(1)[...]).astype(bf16)))
    parts = tuple(jnp.concatenate([turned[0][k], turned[1][k]], 1) for k in range(2))
    mix, bias = (fetch(2)[...], fetch(3)[...]), fetch(4)[:1, :]
    point_chunks(lambda q: tuple(both(part, q) for part in parts), mix, bias, outs[0])
    put(0)


def point_body(near, fetch, outs, put, scratch):
    mix, bias = (fetch(1)[...], fetch(2)[...]), fetch(3)[:1, :]
    state_ref = fetch(0)
    point_chunks(lambda q: split(both(state_ref, q)), mix, bias, outs[0])
    put(0)


def gelu_parts(x):
    square = x * x
    cubic = square * CUBE
    bend = jnp.tanh(x * (cubic + ROOT))
    above = bend + 1.0
    twice = x * above
    slope = above + (twice * (1.0 - bend)) * (cubic * 3.0 + ROOT)
    return twice, slope


def tiles(body, rows=16, lanes=512, height=256, width=2048):
    def step(index, carry):
        start = pl.multiple_of(index * rows, rows)
        for column in range(0, width, lanes):
            body(pl.ds(start, rows), slice(column, column + lanes))
        return carry

    lax.fori_loop(0, height // rows, step, 0)


def one_body(near, fetch, outs, put, scratch):
    send_ref, state_ref, slope_ref = outs
    pre, high, low = scratch
    pre[...] = cells_from(near[0], lambda k: fetch(4 + k), fetch)
    local_ref = fetch(6)

    def body(rows, columns):
        twice, slope = gelu_parts(pre[rows, columns] + local_ref[rows, columns])
        state = 0.5 * twice
        state_ref[rows, columns] = state
        slope_ref[rows, columns] = 0.5 * slope
        high[rows, columns], low[rows, columns] = split(state)

    tiles(body)
    put(1)
    put(2)
    send_modes((high[...], low[...]), [fetch(7), fetch(8)], [fetch(k) for k in range(4)], send_ref)


def two_body(near, fetch, outs, put, scratch):
    send_ref, back_ref = outs
    pre, high, low, hidden, slope_h, slope_l, sums = scratch
    pre[...] = cells_from(near[0], lambda k: fetch(4 + k), fetch)
    local_ref = fetch(6)

    def body(rows, columns):
        twice, slope = gelu_parts(pre[rows, columns] + local_ref[rows, columns])
        pre[rows, columns] = 0.5 * slope
        high[rows, columns], low[rows, columns] = split(0.5 * twice)

    tiles(body)
    up_h, up_l, rows_ref, down_h, down_l, ones_ref, target_ref = [fetch(k) for k in range(9, 16)]

    def chunk(q, carry):
        first = pl.ds(pl.multiple_of(q * 128, 128), 128)
        second = pl.ds(pl.multiple_of(1024 + q * 128, 128), 128)
        left = tuple(jnp.concatenate([part[:, first], part[:, second]], 1) for part in (high, low))
        hidden[...] = dot3(left, (up_h[...], up_l[...]))

        def strip(index, inner):
            rows = pl.ds(pl.multiple_of(index * 16, 16), 16)
            total = jnp.zeros((16, 128), f32)
            for b in range(8):
                columns = slice(b * 128, b * 128 + 128)
                twice, slope = gelu_parts(hidden[rows, columns] + rows_ref[0:16, columns])
                total = total + twice * rows_ref[16:32, columns]
                slope_h[rows, columns], slope_l[rows, columns] = split(slope)
            sums[rows, :128], sums[rows, 128:] = split(total)
            return inner

        lax.fori_loop(0, 16, strip, 0)
        reach = dot3((slope_h[...], slope_l[...]), (down_h[...], down_l[...]), dot_t)
        misfit = dot(sums[:, :128], ones_ref[...]) + dot(sums[:, 128:], ones_ref[...]) - target_ref[:, first]
        for part, columns in ((0, first), (1, second)):
            back = pre[:, columns] * (misfit * reach[:, part * 128 : part * 128 + 128])
            back_ref[:, columns] = back
            high[:, columns], low[:, columns] = split(back)
        return carry

    lax.fori_loop(0, 8, chunk, 0)
    put(1)
    send_modes((high[...], low[...]), [fetch(7), fetch(8)], [fetch(k) for k in range(4)], send_ref)


def back_body(near, fetch, outs, put, scratch):
    pre, high, low = scratch
    pre[...] = cells_from(near[0], lambda k: fetch(4 + k), fetch)
    local_ref, slope_ref = fetch(6), fetch(9)

    def body(rows, columns):
        back = slope_ref[rows, columns] * (pre[rows, columns] + local_ref[rows, columns])
        high[rows, columns], low[rows, columns] = split(back)

    tiles(body)
    send_modes((high[...], low[...]), [fetch(7), fetch(8)], [fetch(k) for k in range(4)], outs[0])


def mode_rows(recv_ref, first, factor, rows_ref):
    spectrum = dot3((first[0][...], first[1][...]), split(recv_ref[...]))
    if factor is not None:
        spectrum = spectrum * factor
    lane = lax.broadcasted_iota(jnp.int32, (64, 128), 1)
    for kz in range(8):
        first = spectrum[:64] if kz == 0 else pltpu.roll(spectrum[:64], 128 - 16 * kz, 1)
        second = spectrum[64:] if kz == 1 else pltpu.roll(spectrum[64:], (144 - 16 * kz) % 128, 1)
        joined = jnp.where(lane < 16, first, jnp.where(lane < 32, second, 0.0))
        rows_ref[pl.ds(kz, 64, stride=8), :] = joined


def selected(rows_ref, table):
    high, low = split(rows_ref[...])
    return dot(high, table[...]) + dot(low, table[...])


def send_cells(sums_ref, factor, first_back, send_ref):
    kz_lane = lax.broadcasted_iota(jnp.int32, (64, 128), 1) // 16
    packed = [jnp.zeros((64, 128), f32) for _ in range(2)]
    for kz in range(8):
        for g in range(2):
            packed[g] = jnp.where(kz_lane == kz, sums_ref[pl.ds(g * 512 + kz, 64, stride=8), :], packed[g])
    joined = jnp.concatenate(packed, 0)
    if factor is not None:
        joined = joined * factor
    send_ref[...] = dot3((first_back[0][...], first_back[1][...]), split(joined))


def mix_body(near, fetch, outs, put, scratch):
    send_ref, rows_ref = outs
    wide, sums, out = scratch
    mode_rows(near[0], [fetch(0), fetch(1)], None, rows_ref)
    put(1)
    wide[...] = selected(rows_ref, fetch(3))
    weight_ref = fetch(4)

    def step(kx, carry):
        real = pl.ds(pl.multiple_of(kx * 8, 8), 8)
        imag = pl.ds(pl.multiple_of(256 + kx * 8, 8), 8)
        total_real = jnp.zeros((8, 128), f32)
        total_imag = jnp.zeros((8, 128), f32)
        for b in range(8):
            columns = slice(b * 128, b * 128 + 128)
            fr, fi = wide[real, columns], wide[imag, columns]
            wr, wi = weight_ref[real, columns], weight_ref[imag, columns]
            total_real = total_real + (fr * wr - fi * wi)
            total_imag = total_imag + (fr * wi + fi * wr)
        sums[real, :] = total_real
        sums[imag, :] = total_imag
        return carry

    lax.fori_loop(0, 32, step, 0, unroll=4)
    mixed = selected(sums, fetch(5))
    out[:512, :] = mixed[:, :128]
    out[512:, :] = mixed[:, 128:]
    send_cells(out, fetch(2)[:1, :], [fetch(6), fetch(7)], send_ref)


def adjoint_body(near, fetch, outs, put, scratch):
    send_ref, rows_ref = outs
    wide, high, low, out = scratch
    mode_rows(near[0], [fetch(0), fetch(1)], fetch(2)[:1, :], rows_ref)
    put(1)
    wide[...] = selected(rows_ref, fetch(3))
    weight_ref = fetch(4)

    def step(kx, carry):
        real = pl.ds(pl.multiple_of(kx * 16, 16), 16)
        imag = pl.ds(pl.multiple_of(256 + kx * 16, 16), 16)
        br, bi = wide[real, :], wide[imag, :]
        for b in range(8):
            columns = slice(b * 128, b * 128 + 128)
            wr, wi = weight_ref[real, columns], weight_ref[imag, columns]
            high[real, columns], low[real, columns] = split(br * wr + bi * wi)
            high[imag, columns], low[imag, columns] = split(bi * wr - br * wi)
        return carry

    lax.fori_loop(0, 16, step, 0)
    table = fetch(5)[...]
    mixed = dot(high[...], table) + dot(low[...], table)
    out[:512, :] = mixed[:, :128]
    out[512:, :] = mixed[:, 128:]
    send_cells(out, None, [fetch(6), fetch(7)], send_ref)


def outer_products(forward_ref, back_ref, spread_ref, tile_ref, grad_ref, wide, narrow):
    wide[...] = selected(forward_ref, spread_ref)
    narrow[...] = selected(back_ref, tile_ref)

    def step(kx, carry):
        real = pl.ds(pl.multiple_of(kx * 8, 8), 8)
        imag = pl.ds(pl.multiple_of(256 + kx * 8, 8), 8)
        br, bi = narrow[real, :], narrow[imag, :]
        for b in range(8):
            columns = slice(b * 128, b * 128 + 128)
            fr, fi = wide[real, columns], wide[imag, columns]
            grad_ref[real, columns] = fr * br + fi * bi
            grad_ref[imag, columns] = fr * bi - fi * br
        return carry

    lax.fori_loop(0, 32, step, 0, unroll=4)


def grad_body(near, fetch, outs, put, scratch):
    outer_products(fetch(0), fetch(1), fetch(2), fetch(3), outs[0], *scratch)
    put(0)


def last_body(near, fetch, outs, put, scratch):
    rows, wide, narrow = scratch
    mode_rows(near[0], [fetch(0), fetch(1)], fetch(2)[:1, :], rows)
    outer_products(fetch(3), rows, fetch(4), fetch(5), outs[0], wide, narrow)
    put(0)


def table_body(near, fetch, outs, put, scratch):
    point_one, point_two, hidden_t, vectors, biases, target, channels, hidden, cells = [fetch(k) for k in range(9)]
    one_h, one_l, two_h, two_l, back_h, back_l, up_h, up_l, down_h, down_l, rows_ref, bias_one, bias_two, target_ref = outs
    z_row = lax.broadcasted_iota(jnp.int32, (256, 1024), 0) // 16 % 8
    z_column = lax.broadcasted_iota(jnp.int32, (256, 1024), 1) // 16 % 8
    same = z_row == z_column

    def widen(left, right, mask, high, low):
        for part, out in zip(split(left), (high, low)):
            rows = dot(channels[...], part).astype(bf16)
            out[...] = jnp.where(mask, right(rows), 0.0).astype(bf16)

    square = same[:, :256]
    to_channels = lambda rows: dot_t(rows, channels[...])
    to_hidden = lambda rows: dot(rows, hidden[...])
    widen(point_one[...].T, to_channels, square, one_h, one_l)
    widen(point_two[...].T, to_channels, square, two_h, two_l)
    widen(point_two[...], to_channels, square, back_h, back_l)
    widen(hidden_t[...], to_hidden, same, up_h, up_l)
    widen(hidden_t[...] * (0.5 * vectors[1:2, :]), to_hidden, same, down_h, down_l)

    def exact(values, product):
        high, low = split(values)
        last = (values - high.astype(f32) - low.astype(f32)).astype(bf16)
        return product(high) + (product(low) + product(last))

    rows_ref[0:16, :] = exact(jnp.broadcast_to(vectors[0:1, :], (16, 128)), to_hidden)
    rows_ref[16:32, :] = exact(jnp.broadcast_to(0.5 * vectors[1:2, :], (16, 128)), to_hidden)
    bias_one[...] = exact(jnp.broadcast_to(biases[0:1, :], (8, 32)), to_channels)
    bias_two[...] = exact(jnp.broadcast_to(biases[1:2, :], (8, 32)), to_channels)
    spread = exact(target[...], lambda part: dot(part, cells[...]))
    target_ref[:128, :] = spread[:, :1024]
    target_ref[128:, :] = spread[:, 1024:]
    for k in range(14):
        put(k)


def shards(
    lifted_field,
    target_field,
    spectral_one,
    spectral_two,
    pointwise_one,
    layer_bias_one,
    pointwise_two,
    layer_bias_two,
    hidden_weight,
    hidden_bias,
    output_weight,
):
    across = tuple(map(jnp.asarray, two_parts(across_table())))
    across_back = tuple(map(jnp.asarray, two_parts(np.ascontiguousarray(across_table().T))))
    depth, depth_lifted = (
        tuple(jnp.asarray(part) for wave in depth_table(major) for part in two_parts(wave)) for major in (False, True)
    )
    first = tuple(map(jnp.asarray, two_parts(first_table())))
    first_back = tuple(map(jnp.asarray, two_parts(np.ascontiguousarray(first_table().T))))
    spread, tile, gather, gather_rows = map(jnp.asarray, selectors())
    channels, hidden, ones, cells = map(jnp.asarray, head_selectors())
    turn = jnp.asarray(turn_table())

    field = lifted_field.reshape(W, 2, 64, 128).transpose(0, 2, 1, 3).reshape(W, 128, 128)
    target = target_field.reshape(2, 64, 128).transpose(1, 0, 2).reshape(128, 128)
    weights_one = spectral_one.reshape(512, 1024)
    weights_two = spectral_two.reshape(512, 1024)
    mine = lax.axis_index("sp")
    lane = jnp.arange(128, dtype=jnp.int32)[None, :]
    factor = jnp.broadcast_to(jnp.where((lane < 16) & (mine % 2 == 0), 1.0, 2.0), (8, 128)).astype(f32)

    def exchange(blocks):
        moved = lax.all_to_all(blocks.reshape(64, 8, 128), "sp", split_axis=0, concat_axis=0, tiled=True)
        return moved.reshape(512, 128)

    block, grid, wide = (512, 128), (256, 2048), (512, 1024)
    vm = pltpu.VMEM
    near_out = (block, f32, "near")
    far_out = lambda shape, kind=f32: (shape, kind, "far")
    work = [vm(grid, f32), vm(grid, bf16), vm(grid, bf16)]
    mix_work = [vm(wide, f32), vm(block, f32), vm((1024, 128), f32)]

    (send,) = run(lift_body, "lift", 2 * 10**9, (), (field, *across, *depth_lifted), [near_out], [])
    recv = exchange(send)
    made = run(
        table_body, "tables", 3 * 10**9, (),
        (
            pointwise_one, pointwise_two, hidden_weight.T, jnp.stack([hidden_bias, output_weight]),
            jnp.stack([layer_bias_one, layer_bias_two]), target, channels, hidden, cells,
        ),
        [far_out((256, 256), bf16)] * 6 + [far_out((256, 1024), bf16)] * 4
        + [far_out((32, 1024)), far_out((8, 256)), far_out((8, 256)), far_out((256, 1024))],
        [],
    )
    mix_one, mix_two, mix_back = made[0:2], made[2:4], made[4:6]
    up, down = made[6:8], made[8:10]
    hidden_rows, bias_one, bias_two, target_wide = made[10:]
    (local_one,) = run(lift_point_body, "lift_point", 4 * 10**9, (), (field, turn, *mix_one, bias_one), [far_out(grid)], [])
    send, modes_one = run(
        mix_body, "mix_one", 10**9, (recv,), (*first, factor, spread, weights_one, gather, *first_back),
        [near_out, far_out(block)], mix_work,
    )
    recv = exchange(send)
    send, state_one, slope_one = run(
        one_body, "grid_one", 5 * 10**9, (recv,), (*depth, *across_back, local_one, *across),
        [near_out, far_out(grid), far_out(grid)], work,
    )
    recv = exchange(send)
    (local_two,) = run(point_body, "point_two", 10**9, (), (state_one, *mix_two, bias_two), [far_out(grid)], [])
    send, modes_two = run(
        mix_body, "mix_two", 10**9, (recv,), (*first, factor, spread, weights_two, gather, *first_back),
        [near_out, far_out(block)], mix_work,
    )
    recv = exchange(send)
    send, back_two = run(
        two_body, "grid_two", 15 * 10**9, (recv,),
        (*depth, *across_back, local_two, *across, *up, hidden_rows, *down, ones, target_wide),
        [near_out, far_out(grid)],
        work + [vm((256, 1024), f32), vm((256, 1024), bf16), vm((256, 1024), bf16), vm((256, 256), bf16)],
    )
    recv = exchange(send)
    no_bias = jnp.zeros((8, 256), f32)
    (local_back,) = run(point_body, "point_back", 10**9, (), (back_two, *mix_back, no_bias), [far_out(grid)], [])
    send, modes_back = run(
        adjoint_body, "adjoint", 10**9, (recv,), (*first, factor, tile, weights_two, gather_rows, *first_back),
        [near_out, far_out(block)], [vm(block, f32), vm(wide, bf16), vm(wide, bf16), vm((1024, 128), f32)],
    )
    recv = exchange(send)
    (gradient_two,) = run(
        grad_body, "grad_two", 10**9, (), (modes_two, modes_back, spread, tile), [far_out(wide)], [vm(wide, f32), vm(block, f32)]
    )
    (send,) = run(
        back_body, "grid_back", 5 * 10**9, (recv,), (*depth, *across_back, local_back, *across, slope_one), [near_out], work
    )
    recv = exchange(send)
    (gradient_one,) = run(
        last_body, "grad_one", 10**9, (recv,), (*first, factor, modes_one, spread, tile), [far_out(wide)],
        [vm(block, f32), vm(wide, f32), vm(block, f32)],
    )
    shape = (2, KX, 8, W * W)
    return (gradient_one.reshape(shape), gradient_two.reshape(shape))


def solution(mesh):
    in_specs = (
        P("batch", "sp", None),
        P("sp", "batch"),
        P(None, None, "sp", None),
        P(None, None, "sp", None),
        P(),
        P(),
        P(),
        P(),
        P(),
        P(),
        P(),
    )
    out_specs = (P("batch", None, "sp", None), P("batch", None, "sp", None))
    return jax.shard_map(shards, mesh=mesh, in_specs=in_specs, out_specs=out_specs, check_vma=False)
```

time: 724 us -> 206 us (0.28); the launches traced: 716 us -> 206 us
  local copies, waits for them, and re-layouts: 405 us -> 1.21 us
  matrix products: 185 us -> 0 us
  Pallas kernels: 0 us -> 90.1 us
  other arithmetic: 17.8 us -> 1.16 us
    unnamed x44 -> x8, local copies, waits for them, and re-layouts: 211 us -> 0.02 us
    dot_general x39 -> x0, matrix products: 185 us -> none  [product(): jnp.einsum(form, left_operand, right_operand, precision=precise, preferre...]
    reshape x17 -> x0, local copies, waits for them, and re-layouts: 105 us -> none  [the longest x4 70.4 us: to_modes(): slab_data = across_spectra.reshape(rows_here, 2, KY * KZ * channels)]
    pallas_call x0 -> x13, Pallas kernels: none -> 90.1 us  [run(): pl.pallas_call(kernel, in_specs=[vmem] * len(near) + [hbm] * len(far), ou...]
    all_to_all x16 -> x0, local copies, waits for them, and re-layouts: 55.9 us -> none  [the longest x13 55.7 us: to_modes(): lax.all_to_all(slab_data, 'sp', split_axis=2, concat_axis=0, tiled=True)]
    another operation x10 -> x0, local copies, waits for them, and re-layouts: 15.6 us -> none  [the longest x4 15 us: weight_gradient(): stacked = jnp.stack([real_grad, imag_grad], 0)]
    squeeze x18 -> x0, local copies, waits for them, and re-layouts: 12.2 us -> none  [the longest x2 5.56 us: apply_modes(): weights[1]]
    add x5 -> x0, other arithmetic: 9.29 us -> none  [the longest x2 9.23 us: weight_gradient(): product('xmi,xmo->xmio', forward_spectrum[0], back_spectrum[0])]
  transfers between devices with their start and end apart: 5 -> 5, of which waited for: 4 -> 5; matrix products, arithmetic and copies ran while one was open for 4% -> 1% of each run, Pallas kernels for 0% -> 12%
where the time goes in v1:
time: 206 us
  Pallas kernels  90.1 us (44%)
  waiting for transfers between devices  40.2 us (20%)
  blocking collectives  39.9 us (19%)
  starting transfers between devices  31.9 us (15%)
    pallas_call x13, Pallas kernels, run(): pl.pallas_call(kernel, in_specs=[vmem] * len(near) + [hbm] * len(far), ou...  90.1 us
    all_to_all x5, waiting for transfers between devices, exchange(): lax.all_to_all(blocks.reshape(64, 8, 128), 'sp', split_axis=0, concat_axi...  40.2 us
    all_to_all x2, blocking collectives, exchange(): lax.all_to_all(blocks.reshape(64, 8, 128), 'sp', split_axis=0, concat_axi...  39.9 us
    all_to_all x5, starting transfers between devices, exchange(): lax.all_to_all(blocks.reshape(64, 8, 128), 'sp', split_axis=0, concat_axi...  31.9 us
  transfers between devices with their start and end apart: 5, of which 5 were waited for; matrix products, arithmetic and copies ran while one was open for 1% of the time, Pallas kernels for 12%

profile of v1, /device:TPU:1, one launch (start us, length us, event | category | flops | bytes accessed | tf_op | source)
XLA Modules:
  0.0 205.6 jit_solution(3035750462092948139)
XLA Ops:
  0.7 4.6 %lift.1 = f32[512,128]{1,0:T(8,128)} custom-call(f32[32,128,128]{2,1,0:T(8,128)} %bitcast.47, bf16[128,256]{1,0:T(8,128)(2,1)} %constant.78.clone.refs_1_.refs_8_, bf16[128,256]{1,0:T(8,128)(2,1)} %constant.79.clone.refs_2_.refs_9_, bf16[1024,256]{1,0:T(8,128)(2,1)} %constant.86.clone.refs_3_, bf16[1024,256]{1,0:T(8,128)(2,1)} %constant.87.clone.refs_4_, ...), custom_call_target="tpu_custom_call" | custom-call | flops 2000000000 | bytes 4325376 | tf_op jit(solution)/shard_map/lift/pallas_call | solution.py:140
  5.3 13.0 %all-to-all-start = ((f32[64,8,128]{2,1,0:T(8,128)}), f32[64,8,128]{2,1,0:T(8,128)S(1)}, u32[]{:S(2)}, u32[]{:S(2)}) async-start(f32[64,8,128]{2,1,0:T(8,128)} %bitcast.3), calls=%async_computation | async-start | bytes 524288 | tf_op jit(solution)/shard_map/all_to_all | solution.py:531
  19.5 12.0 %all-to-all-done = f32[64,8,128]{2,1,0:T(8,128)S(1)} async-done(((f32[64,8,128]{2,1,0:T(8,128)}), f32[64,8,128]{2,1,0:T(8,128)S(1)}, u32[]{:S(2)}, u32[]{:S(2)}) %all-to-all-start) | async-done | bytes 262176 | tf_op jit(solution)/shard_map/all_to_all | solution.py:531
  32.1 4.0 %mix_one.1 = (f32[512,128]{1,0:T(8,128)}, f32[512,128]{1,0:T(8,128)}) custom-call(f32[512,128]{1,0:T(8,128)S(1)} %bitcast.33, bf16[128,512]{1,0:T(8,128)(2,1)} %constant.90.clone.refs_1_, bf16[128,512]{1,0:T(8,128)(2,1)} %constant.91.clone.refs_2_, f32[8,128]{1,0:T(8,128)} %broadcast_in_dim.19.refs_3_, ...), custom_call_target="tpu_custom_call" | custom-call | flops 1000000000 | bytes 3215360 | tf_op jit(solution)/shard_map/mix_one/pallas_call | solution.py:140
  36.1 4.7 %all-to-all-start.1 = ((f32[64,8,128]{2,1,0:T(8,128)}), f32[64,8,128]{2,1,0:T(8,128)S(1)}, u32[]{:S(2)}, u32[]{:S(2)}) async-start(f32[64,8,128]{2,1,0:T(8,128)} %bitcast.6), calls=%async_computation.1 | async-start | bytes 524288 | tf_op jit(solution)/shard_map/all_to_all | solution.py:531
  40.8 5.2 %tables.1 = (bf16[256,256]{1,0:T(8,128)(2,1)}, bf16[256,256]{1,0:T(8,128)(2,1)}, bf16[256,256]{1,0:T(8,128)(2,1)}, bf16[256,256]{1,0:T(8,128)(2,1)}, bf16[256,25...) custom-call(f32[32,32]{1,0:T(8,128)} %refs_0_.1, ...), custom_call_target="tpu_custom_call" | custom-call | flops 3000000000 | bytes 894208 | tf_op jit(solution)/shard_map/tables/pallas_call | solution.py:140
  46.0 6.9 %lift_point.1.refs_7_ = f32[256,2048]{1,0:T(8,128)} custom-call(f32[32,128,128]{2,1,0:T(8,128)} %bitcast.48, bf16[1024,1024]{1,0:T(8,128)(2,1)} %constant.102.clone.refs_1_, bf16[256,256]{1,0:T(8,128)(2,1)} %get-tuple-element.28.refs_2_, bf16[256,256]{1,0:T(8,128)(2,1)} %get-tuple-element.29.refs_3_, f32[8,256]{1,0:T(8,128)} %get-tuple-element.30.refs_4_), custom_call_target="tpu_custom_call" | custom-call | flops 4000000000 | bytes 4464640 | tf_op jit(solution)/shard_map/lift_point/pallas_call | solution.py:140
  54.0 8.3 %grid_one.1 = (f32[512,128]{1,0:T(8,128)S(1)}, f32[256,2048]{1,0:T(8,128)}, f32[256,2048]{1,0:T(8,128)}) custom-call(f32[512,128]{1,0:T(8,128)S(1)} %bitcast.34, bf16[1024,256]{1,0:T(8,128)(2,1)} %constant.82.clone.refs_1_, bf16[1024,256]{1,0:T(8,128)(2,1)} %constant.83.clone.refs_2_, bf16[1024,256]{1,0:T(8,128)(2,1)} %constant.84.clone.refs_3_, ...), custom_call_target="tpu_custom_call" | custom-call | flops 5000000000 | bytes 4718592 | tf_op jit(solution)/shard_map/grid_one/pallas_call | solution.py:140
  62.2 22.3 %all_to_all.35 = f32[64,8,128]{2,1,0:T(8,128)S(1)} all-to-all(f32[64,8,128]{2,1,0:T(8,128)S(1)} %bitcast.40), channel_id=1, replica_groups=mesh['sp'=64,'batch'=4] {'sp'}, dimensions={0} | all-to-all | bytes 524288 | tf_op jit(solution)/shard_map/all_to_all | solution.py:531
  84.5 4.0 %mix_two.1 = (f32[512,128]{1,0:T(8,128)}, f32[512,128]{1,0:T(8,128)}) custom-call(f32[512,128]{1,0:T(8,128)S(1)} %bitcast.41, bf16[128,512]{1,0:T(8,128)(2,1)} %constant.90.clone.refs_1_, bf16[128,512]{1,0:T(8,128)(2,1)} %constant.91.clone.refs_2_, f32[8,128]{1,0:T(8,128)} %broadcast_in_dim.19.refs_3_, ...), custom_call_target="tpu_custom_call" | custom-call | flops 1000000000 | bytes 3215360 | tf_op jit(solution)/shard_map/mix_two/pallas_call | solution.py:140
  88.5 4.7 %all-to-all-start.3 = ((f32[64,8,128]{2,1,0:T(8,128)}), f32[64,8,128]{2,1,0:T(8,128)S(1)}, u32[]{:S(2)}, u32[]{:S(2)}) async-start(f32[64,8,128]{2,1,0:T(8,128)} %bitcast.21), calls=%async_computation.3 | async-start | bytes 524288 | tf_op jit(solution)/shard_map/all_to_all | solution.py:531
  93.3 4.0 %point_two.1.refs_7_ = f32[256,2048]{1,0:T(8,128)} custom-call(f32[256,2048]{1,0:T(8,128)} %get-tuple-element.33.refs_0_, bf16[256,256]{1,0:T(8,128)(2,1)} %get-tuple-element.34.refs_1_, bf16[256,256]{1,0:T(8,128)(2,1)} %get-tuple-element.35.refs_2_, f32[8,256]{1,0:T(8,128)} %get-tuple-element.36.refs_3_), custom_call_target="tpu_custom_call" | custom-call | flops 1000000000 | bytes 2367488 | tf_op jit(solution)/shard_map/point_two/pallas_call | solution.py:140
  97.2 9.2 %all-to-all-done.3 = f32[64,8,128]{2,1,0:T(8,128)S(1)} async-done(((f32[64,8,128]{2,1,0:T(8,128)}), f32[64,8,128]{2,1,0:T(8,128)S(1)}, u32[]{:S(2)}, u32[]{:S(2)}) %all-to-all-start.3) | async-done | bytes 262176 | tf_op jit(solution)/shard_map/all_to_all | solution.py:531
  106.4 29.0 %grid_two.1 = (f32[512,128]{1,0:T(8,128)S(1)}, f32[256,2048]{1,0:T(8,128)}) custom-call(f32[512,128]{1,0:T(8,128)S(1)} %bitcast.36, bf16[1024,256]{1,0:T(8,128)(2,1)} %constant.82.clone.refs_1_, bf16[1024,256]{1,0:T(8,128)(2,1)} %constant.83.clone.refs_2_, bf16[1024,256]{1,0:T(8,128)(2,1)} %constant.84.clone.refs_3_, ...), custom_call_target="tpu_custom_call" | custom-call | flops 15000000512 | bytes 8028160 | tf_op jit(solution)/shard_map/grid_two/pallas_call | solution.py:140
  135.5 17.7 %all_to_all.36 = f32[64,8,128]{2,1,0:T(8,128)S(1)} all-to-all(f32[64,8,128]{2,1,0:T(8,128)S(1)} %bitcast.38), channel_id=1, replica_groups=mesh['sp'=64,'batch'=4] {'sp'}, dimensions={0} | all-to-all | bytes 524288 | tf_op jit(solution)/shard_map/all_to_all | solution.py:531
  153.1 4.5 %adjoint.1 = (f32[512,128]{1,0:T(8,128)}, f32[512,128]{1,0:T(8,128)}) custom-call(f32[512,128]{1,0:T(8,128)S(1)} %bitcast.39, bf16[128,512]{1,0:T(8,128)(2,1)} %constant.90.clone.refs_1_, bf16[128,512]{1,0:T(8,128)(2,1)} %constant.91.clone.refs_2_, f32[8,128]{1,0:T(8,128)} %broadcast_in_dim.19.refs_3_, ...), custom_call_target="tpu_custom_call" | custom-call | flops 1000000000 | bytes 3444736 | tf_op jit(solution)/shard_map/adjoint/pallas_call | solution.py:140
  157.6 4.7 %all-to-all-start.5 = ((f32[64,8,128]{2,1,0:T(8,128)}), f32[64,8,128]{2,1,0:T(8,128)S(1)}, u32[]{:S(2)}, u32[]{:S(2)}) async-start(f32[64,8,128]{2,1,0:T(8,128)} %bitcast.25), calls=%async_computation.5 | async-start | bytes 524288 | tf_op jit(solution)/shard_map/all_to_all | solution.py:531
  162.9 4.0 %point_back.1.refs_7_ = f32[256,2048]{1,0:T(8,128)} custom-call(f32[256,2048]{1,0:T(8,128)} %get-tuple-element.45.refs_0_, bf16[256,256]{1,0:T(8,128)(2,1)} %get-tuple-element.46.refs_1_, bf16[256,256]{1,0:T(8,128)(2,1)} %get-tuple-element.47.refs_2_, f32[8,256]{1,0:T(8,128)} %broadcast_in_dim.20.refs_3_), custom_call_target="tpu_custom_call" | custom-call | flops 1000000000 | bytes 2367488 | tf_op jit(solution)/shard_map/point_back/pallas_call | solution.py:140
  166.9 8.6 %all-to-all-done.5 = f32[64,8,128]{2,1,0:T(8,128)S(1)} async-done(((f32[64,8,128]{2,1,0:T(8,128)}), f32[64,8,128]{2,1,0:T(8,128)S(1)}, u32[]{:S(2)}, u32[]{:S(2)}) %all-to-all-start.5) | async-done | bytes 262176 | tf_op jit(solution)/shard_map/all_to_all | solution.py:531
  175.5 8.0 %grid_back.1 = f32[512,128]{1,0:T(8,128)} custom-call(f32[512,128]{1,0:T(8,128)S(1)} %bitcast.35, bf16[1024,256]{1,0:T(8,128)(2,1)} %constant.82.clone.refs_1_, bf16[1024,256]{1,0:T(8,128)(2,1)} %constant.83.clone.refs_2_, bf16[1024,256]{1,0:T(8,128)(2,1)} %constant.84.clone.refs_3_, bf16[1024,256]{1,0:T(8,128)(2,1)} %constant.85.clone.refs_4_, ...), custom_call_target="tpu_custom_call" | custom-call | flops 5000000000 | bytes 6815744 | tf_op jit(solution)/shard_map/grid_back/pallas_call | solution.py:140
  183.5 4.7 %all-to-all-start.6 = ((f32[64,8,128]{2,1,0:T(8,128)}), f32[64,8,128]{2,1,0:T(8,128)S(1)}, u32[]{:S(2)}, u32[]{:S(2)}) async-start(f32[64,8,128]{2,1,0:T(8,128)} %bitcast.27), calls=%async_computation.6 | async-start | bytes 524288 | tf_op jit(solution)/shard_map/all_to_all | solution.py:531
  188.3 3.6 %grad_two.1 = f32[512,1024]{1,0:T(8,128)} custom-call(f32[512,128]{1,0:T(8,128)} %get-tuple-element.50.refs_0_, f32[512,128]{1,0:T(8,128)} %get-tuple-element.51.refs_1_, bf16[128,1024]{1,0:T(8,128)(2,1)} %constant.94.clone.refs_4_.refs_5_.refs_2_, bf16[128,128]{1,0:T(8,128)(2,1)} %constant.95.clone.refs_4_.refs_6_.refs_3_), custom_call_target="tpu_custom_call" | custom-call | flops 1000000000 | bytes 819200 | tf_op jit(solution)/shard_map/grad_two/pallas_call | solution.py:140
  191.9 9.5 %all-to-all-done.6 = f32[64,8,128]{2,1,0:T(8,128)S(1)} async-done(((f32[64,8,128]{2,1,0:T(8,128)}), f32[64,8,128]{2,1,0:T(8,128)S(1)}, u32[]{:S(2)}, u32[]{:S(2)}) %all-to-all-start.6) | async-done | bytes 262176 | tf_op jit(solution)/shard_map/all_to_all | solution.py:531
  201.4 3.9 %grad_one.1 = f32[512,1024]{1,0:T(8,128)} custom-call(f32[512,128]{1,0:T(8,128)S(1)} %bitcast.37, bf16[128,512]{1,0:T(8,128)(2,1)} %constant.90.clone.refs_1_, bf16[128,512]{1,0:T(8,128)(2,1)} %constant.91.clone.refs_2_, f32[8,128]{1,0:T(8,128)} %broadcast_in_dim.19.refs_3_, f32[512,128]{1,0:T(8,128)} %get-tuple-element.49.refs_4_, ...), custom_call_target="tpu_custom_call" | custom-call | flops 1000000000 | bytes 1085440 | tf_op jit(solution)/shard_map/grad_one/pallas_call | solution.py:140
  (14 shorter events, 3.4 us)
Async XLA Ops:
  0.6 17.7 %copy-start = (f32[128]{0:T(128)S(1)}, f32[128]{0:T(128)}, u32[]{:S(2)}) copy-start(f32[128]{0:T(128)} %param.46) | copy-start | bytes 1540
  0.6 17.7 %copy-start.1 = (f32[128]{0:T(128)S(1)}, f32[128]{0:T(128)}, u32[]{:S(2)}) copy-start(f32[128]{0:T(128)} %param.45) | copy-start | bytes 1540
  0.7 18.3 %copy-start.2 = (f32[32]{0:T(128)S(1)}, f32[32]{0:T(128)}, u32[]{:S(2)}) copy-start(f32[32]{0:T(128)} %param.43) | copy-start | bytes 388
  0.7 18.2 %copy-start.3 = (f32[32]{0:T(128)S(1)}, f32[32]{0:T(128)}, u32[]{:S(2)}) copy-start(f32[32]{0:T(128)} %param.41) | copy-start | bytes 388
  5.3 26.2 %all-to-all-start = ((f32[64,8,128]{2,1,0:T(8,128)}), f32[64,8,128]{2,1,0:T(8,128)S(1)}, u32[]{:S(2)}, u32[]{:S(2)}) async-start(f32[64,8,128]{2,1,0:T(8,128)} %bitcast.3), calls=%async_computation | async-start | bytes 524288 | tf_op jit(solution)/shard_map/all_to_all | solution.py:531
  36.1 17.9 %all-to-all-start.1 = ((f32[64,8,128]{2,1,0:T(8,128)}), f32[64,8,128]{2,1,0:T(8,128)S(1)}, u32[]{:S(2)}, u32[]{:S(2)}) async-start(f32[64,8,128]{2,1,0:T(8,128)} %bitcast.6), calls=%async_computation.1 | async-start | bytes 524288 | tf_op jit(solution)/shard_map/all_to_all | solution.py:531
  88.5 17.9 %all-to-all-start.3 = ((f32[64,8,128]{2,1,0:T(8,128)}), f32[64,8,128]{2,1,0:T(8,128)S(1)}, u32[]{:S(2)}, u32[]{:S(2)}) async-start(f32[64,8,128]{2,1,0:T(8,128)} %bitcast.21), calls=%async_computation.3 | async-start | bytes 524288 | tf_op jit(solution)/shard_map/all_to_all | solution.py:531
  157.6 17.9 %all-to-all-start.5 = ((f32[64,8,128]{2,1,0:T(8,128)}), f32[64,8,128]{2,1,0:T(8,128)S(1)}, u32[]{:S(2)}, u32[]{:S(2)}) async-start(f32[64,8,128]{2,1,0:T(8,128)} %bitcast.25), calls=%async_computation.5 | async-start | bytes 524288 | tf_op jit(solution)/shard_map/all_to_all | solution.py:531
  183.5 17.9 %all-to-all-start.6 = ((f32[64,8,128]{2,1,0:T(8,128)}), f32[64,8,128]{2,1,0:T(8,128)S(1)}, u32[]{:S(2)}, u32[]{:S(2)}) async-start(f32[64,8,128]{2,1,0:T(8,128)} %bitcast.27), calls=%async_computation.6 | async-start | bytes 524288 | tf_op jit(solution)/shard_map/all_to_all | solution.py:531
